TPU v7x, 256 devices: a whole 4x4x8 slice. The times are simulated.
256 devices in a mesh: resp: 8 (over y, x_hi), expert: 16 (over z, x_lo), group: 2 (over core).
Axes of the slice: x: 4 (x_hi: 2, x_lo: 2; x = x_hi * 2 + x_lo), y: 4, z: 8, core: 2. Of those that a mesh axis runs over, the one named last changes fastest.
Arguments:
- tokens: bfloat16 [32768, 4096], P(('group', 'resp', 'expert')), parts along dimension 0, may hold values from -6 to 6
- cotangent: bfloat16 [32768, 4096], P(('group', 'resp', 'expert')), parts along dimension 0, may hold values from -6 to 6
- expert_ids: int32 [32768, 1], P(('group', 'resp', 'expert')), parts along dimension 0, may hold values from 0 to 15; in each aligned block of 128 rows (0 to 127, 128 to 255, ...) at most 9 rows name the same one
- gate_weights: float32 [32768, 1], P(('group', 'resp', 'expert')), parts along dimension 0, may hold values from 0.05 to 1
- gate_proj: bfloat16 [16, 1536, 4096], P('expert', 'resp'), may hold values from -0.09375 to 0.09375
- up_proj: bfloat16 [16, 1536, 4096], P('expert', 'resp'), may hold values from -0.09375 to 0.09375
- down_proj: bfloat16 [16, 1536, 4096], P('expert', 'resp'), may hold values from -0.15625 to 0.15625
Outputs:
- token_grad: bfloat16 [32768, 4096], P(('group', 'resp', 'expert')), parts along dimension 0
- gate_proj_grad: bfloat16 [32, 1536, 4096], P(('group', 'expert'), 'resp'), parts along dimension 0
- up_proj_grad: bfloat16 [32, 1536, 4096], P(('group', 'expert'), 'resp'), parts along dimension 0
- down_proj_grad: bfloat16 [32, 1536, 4096], P(('group', 'expert'), 'resp'), parts along dimension 0
There are 2 independent parts, one for each index of `group`. A program takes and returns all parts, laid end to end along the dimension named above; an argument that names none is the same for every part. Nothing has to cross between parts.
Inputs may be any that keep to these rules, and one draw needn't show every extreme that they name: `expert_ids`: among the 128 tokens of one device no expert is named more than 9 times, and in every draw some device names some expert exactly 9 times.
All inputs are finite; a program needn't handle non-finite values.
Results may differ from a plain program's by a relative error of at most 0.017.
Values may be sent and summed in bfloat16 or wider, within the bound.
A program may use at most 192 MiB of HBM per device.

v0:
```python
import jax
import jax.numpy as jnp
from jax import lax
from jax.sharding import PartitionSpec as P


def expert_pass(x_rows, g_rows, w_gate, w_up, w_down):
    gate_pre = jnp.dot(x_rows, w_gate.T, preferred_element_type=jnp.float32)
    up_pre = jnp.dot(x_rows, w_up.T, preferred_element_type=jnp.float32)
    sigmoid_a = jax.nn.sigmoid(gate_pre)
    activated = gate_pre * sigmoid_a
    hidden = (activated * up_pre).astype(jnp.bfloat16)
    hidden_grad = jnp.dot(g_rows, w_down.T, preferred_element_type=jnp.float32)
    slope = sigmoid_a * (1.0 + gate_pre * (1.0 - sigmoid_a))
    gate_grad = (hidden_grad * up_pre * slope).astype(jnp.bfloat16)
    up_grad = (hidden_grad * activated).astype(jnp.bfloat16)
    down_total = jnp.dot(hidden.T, g_rows, preferred_element_type=jnp.float32).astype(jnp.bfloat16)
    gate_total = jnp.dot(gate_grad.T, x_rows, preferred_element_type=jnp.float32).astype(
        jnp.bfloat16
    )
    up_total = jnp.dot(up_grad.T, x_rows, preferred_element_type=jnp.float32).astype(jnp.bfloat16)
    return (gate_grad, up_grad, gate_total, up_total, down_total)


def local(tokens, cotangent, expert_ids, gate_weights, gate_proj, up_proj, down_proj):
    experts = lax.axis_size("expert")
    tok_rows = tokens.shape[0]
    model_width = tokens.shape[1]
    capacity = tok_rows // experts + max(1, tok_rows // (8 * experts))
    chosen = expert_ids[:, 0]
    onehot = (chosen[:, None] == jnp.arange(experts, dtype=jnp.int32)[None, :]).astype(jnp.int32)
    rank_rows = jnp.cumsum(onehot, axis=0) - onehot
    slot_index = jnp.sum(rank_rows * onehot, axis=1)
    target = chosen * capacity + slot_index
    scaled = (gate_weights * cotangent.astype(jnp.float32)).astype(jnp.bfloat16)
    send_rows = jnp.zeros((experts * capacity, model_width), jnp.bfloat16).at[target].set(tokens)
    send_grads = jnp.zeros((experts * capacity, model_width), jnp.bfloat16).at[target].set(scaled)
    w_gate = gate_proj[0]
    w_up = up_proj[0]
    w_down = down_proj[0]
    part_rows, part_grads = (
        lax.all_to_all(
            send_rows.reshape(experts, capacity, model_width),
            "expert",
            split_axis=0,
            concat_axis=0,
            tiled=True,
        ),
        lax.all_to_all(
            send_grads.reshape(experts, capacity, model_width),
            "expert",
            split_axis=0,
            concat_axis=0,
            tiled=True,
        ),
    )
    gathered, grad_rows = (
        lax.all_gather(
            part_rows.reshape(experts * capacity, model_width), "resp", axis=0, tiled=True
        ),
        lax.all_gather(
            part_grads.reshape(experts * capacity, model_width), "resp", axis=0, tiled=True
        ),
    )
    gate_grad, up_grad, gate_total, up_total, down_total = expert_pass(
        gathered, grad_rows, w_gate, w_up, w_down
    )
    term = jnp.dot(gate_grad, w_gate, preferred_element_type=jnp.float32)
    own_sums = lax.psum_scatter(
        (term + jnp.dot(up_grad, w_up, preferred_element_type=jnp.float32)).astype(jnp.bfloat16),
        "resp",
        scatter_dimension=0,
        tiled=True,
    )
    combined = lax.all_to_all(
        own_sums.reshape(experts, capacity, model_width),
        "expert",
        split_axis=0,
        concat_axis=0,
        tiled=True,
    )
    combined = combined.reshape(experts * capacity, model_width)
    token_grad = combined[target]
    return (token_grad, gate_total[None], up_total[None], down_total[None])


def solution(mesh):
    in_specs = (
        P(("group", "resp", "expert"), None),
        P(("group", "resp", "expert"), None),
        P(("group", "resp", "expert"), None),
        P(("group", "resp", "expert"), None),
        P("expert", "resp", None),
        P("expert", "resp", None),
        P("expert", "resp", None),
    )
    out_specs = (
        P(("group", "resp", "expert"), None),
        P(("group", "expert"), "resp", None),
        P(("group", "expert"), "resp", None),
        P(("group", "expert"), "resp", None),
    )
    return jax.shard_map(local, mesh=mesh, in_specs=in_specs, out_specs=out_specs, check_vma=False)
```

profile of v0, /device:TPU:25, one launch (start us, length us, event | category | flops | bytes accessed | tf_op | source)
XLA Modules:
  0.0 549.1 jit_solution(3435960604517829540)
XLA Ops:
  7.2 0.0 copy-start
  7.2 0.0 all-gather.5.cloned.1.call-start
  7.2 0.8 fusion.20
  8.1 0.2 reduce_window_sum.11
  8.3 0.8 select_reduce_fusion
  9.1 0.7 fusion.21
  9.8 3.0 scatter_custom_fusion.1
  12.8 1.6 reshape.29
  14.4 58.6 %all_to_all.15 = bf16[16,9,4096]{2,1,0:T(8,128)(2,1)} all-to-all(bf16[16,9,4096]{2,1,0:T(8,128)(2,1)} %reshape.29), channel_id=1, replica_groups=mesh['resp'=8,'expert'=16,'group'=2] {'expert'}, dimensions={0} | all-to-all | bytes 2359296 | tf_op jit(solution)/shard_map/all_to_all | solution.py:42
  73.0 0.0 copy-start.7
  73.0 2.6 reshape.30
  75.7 0.0 all-gather.5.cloned.1.call-update
  75.7 0.0 all-gather.3.cloned.1.call-start
  75.7 0.0 copy-done.7
  75.7 3.1 scatter_custom_fusion
  78.9 1.6 reshape.27
  80.5 53.4 %all_to_all.16 = bf16[16,9,4096]{2,1,0:T(8,128)(2,1)} all-to-all(bf16[16,9,4096]{2,1,0:T(8,128)(2,1)} %reshape.27), channel_id=1, replica_groups=mesh['resp'=8,'expert'=16,'group'=2] {'expert'}, dimensions={0} | all-to-all | bytes 2359296 | tf_op jit(solution)/shard_map/all_to_all | solution.py:49
  133.9 2.6 reshape.28
  136.5 0.0 all-gather.3.cloned.1.call-update
  136.5 0.0 copy-start.2
  136.5 0.2 reduce-scatter.2.cloned.1.call-start
  136.8 68.4 %all-gather.5.cloned.1.call-done = bf16[1152,4096]{1,0:T(8,128)(2,1)} async-done(((bf16[144,4096]{1,0:T(8,128)(2,1)}), bf16[1152,4096]{1,0:T(8,128)(2,1)}) %all-gather.5.cloned.1.call-update) | async-done | bytes 9437200 | tf_op jit(solution)/shard_map/all_gather | solution.py:58
  205.2 0.0 copy-done
  205.2 0.0 copy-start.8
  205.2 8.0 %fusion.6 = f32[1152,192]{0,1:T(8,128)} fusion(bf16[1152,4096]{1,0:T(8,128)(2,1)} %all-gather.5.cloned.1.call-done, bf16[1,192,4096]{2,1,0:T(8,128)(2,1)S(1)} %copy-done), kind=kOutput, calls=%fused_computation.14 | convolution fusion | flops 1811939328 | bytes 11894784 | tf_op jit(solution)/shard_map/dot_general | solution.py:8
  213.2 0.0 copy-done.2
  213.2 0.0 copy-done.8
  213.2 4.2 fusion.9
  217.4 110.5 %all-gather.3.cloned.1.call-done = bf16[1152,4096]{1,0:T(8,128)(2,1)} async-done(((bf16[144,4096]{1,0:T(8,128)(2,1)}), bf16[1152,4096]{1,0:T(8,128)(2,1)}) %all-gather.3.cloned.1.call-update) | async-done | bytes 9437200 | tf_op jit(solution)/shard_map/all_gather | solution.py:61
  327.9 8.0 %multiply_convert_fusion.3 = (bf16[1152,192]{0,1:T(8,128)(2,1)S(1)}, bf16[1152,192]{0,1:T(8,128)(2,1)S(1)}) fusion(f32[1152,192]{0,1:T(8,128)} %fusion.6, f32[1152,192]{0,1:T(8,128)} %fusion.9, bf16[1152,4096]{1,0:T(8,128)(2,1)} %all-gather.3.cloned.1.call-done, bf16[1,192,4096]{2,1,0:T(8,128)(2,1)} %param.13), kind=kOutput, calls=%fused_computation.24 | convolution fusion | flops 1814814720 | bytes 13664256 | tf_op jit(solution)/shard_map/dot_general | solution.py:13
  335.9 0.0 copy-start.3
  335.9 0.0 copy-start.5
  335.9 7.9 %fusion.4 = f32[1152,4096]{1,0:T(8,128)} fusion(bf16[1152,192]{0,1:T(8,128)(2,1)S(1)} %get-tuple-element.5, bf16[1,192,4096]{2,1,0:T(8,128)(2,1)S(1)} %copy-done), kind=kOutput, calls=%fused_computation.12 | convolution fusion | flops 1811939328 | bytes 20889600 | tf_op jit(solution)/shard_map/dot_general | solution.py:68
  343.8 0.0 copy-done.3
  343.8 0.0 copy-done.5
  343.8 10.7 %fusion = bf16[1152,4096]{1,0:T(8,128)(2,1)} fusion(f32[1152,4096]{1,0:T(8,128)} %fusion.4, bf16[1152,192]{0,1:T(8,128)(2,1)S(1)} %get-tuple-element.4, bf16[1,192,4096]{2,1,0:T(8,128)(2,1)S(1)} %copy-done.2), kind=kOutput, calls=%fused_computation.4 | convolution fusion | flops 1821376512 | bytes 30326784 | tf_op jit(solution)/shard_map/dot_general | solution.py:70
  354.5 0.0 reduce-scatter.2.cloned.1.call-update
  354.5 126.4 %reduce-scatter.2.cloned.1.call-done = bf16[144,4096]{1,0:T(8,128)(2,1)} async-done(((bf16[1152,4096]{1,0:T(8,128)(2,1)}), bf16[144,4096]{1,0:T(8,128)(2,1)}) %reduce-scatter.2.cloned.1.call-update) | async-done | bytes 1179664 | tf_op jit(solution)/shard_map/reduce_scatter | solution.py:69
  480.9 2.6 reshape.31
  483.5 0.0 copy-start.6
  483.5 7.1 %all-to-all-start.2 = ((bf16[16,9,4096]{2,1,0:T(8,128)(2,1)}), bf16[16,9,4096]{2,1,0:T(8,128)(2,1)}, u32[]{:S(2)}, u32[]{:S(2)}) async-start(bf16[16,9,4096]{2,1,0:T(8,128)(2,1)} %reshape.31), calls=%async_computation.3 | async-start | bytes 4194304 | tf_op jit(solution)/shard_map/all_to_all | solution.py:75
  490.6 0.0 copy-done.6
  490.6 0.0 copy-start.4
  490.6 0.0 slice-start
  490.7 0.0 slice-start.1
  490.7 7.2 %fusion.2 = bf16[1,192,4096]{2,1,0:T(8,128)(2,1)} fusion(bf16[1152,192]{0,1:T(8,128)(2,1)S(1)} %copy-done.6, bf16[1152,4096]{1,0:T(8,128)(2,1)} %all-gather.5.cloned.1.call-done), kind=kOutput, calls=%fused_computation.9 | convolution fusion | flops 1812725760 | bytes 11452416 | tf_op jit(solution)/shard_map/dot_general | solution.py:21
  497.9 0.0 copy-done.4
  497.9 0.0 slice-start.2
  497.9 0.0 copy-start.9
  497.9 0.0 copy-start.10
  497.9 7.2 %fusion.1 = bf16[1,192,4096]{2,1,0:T(8,128)(2,1)} fusion(bf16[1152,192]{0,1:T(8,128)(2,1)S(1)} %copy-done.4, bf16[1152,4096]{1,0:T(8,128)(2,1)} %all-gather.5.cloned.1.call-done), kind=kOutput, calls=%fused_computation.8 | convolution fusion | flops 1812725760 | bytes 11452416 | tf_op jit(solution)/shard_map/dot_general | solution.py:18
  505.0 0.0 slice-done
  505.1 0.0 slice-done.1
  505.1 0.0 slice-done.2
  505.1 0.0 copy-done.9
  505.1 0.0 copy-done.10
  505.1 3.4 fusion.3
  508.5 30.1 %all-to-all-done.2 = bf16[16,9,4096]{2,1,0:T(8,128)(2,1)} async-done(((bf16[16,9,4096]{2,1,0:T(8,128)(2,1)}), bf16[16,9,4096]{2,1,0:T(8,128)(2,1)}, u32[]{:S(2)}, u32[]{:S(2)}) %all-to-all-start.2) | async-done | bytes 1179680 | tf_op jit(solution)/shard_map/all_to_all | solution.py:75
  538.6 1.8 reshape.32
  540.4 0.0 copy-start.1
  540.4 2.2 gather_fusion
  542.6 0.0 copy-done.1
  (2 shorter events, 0.0 us)
Async XLA Ops:
  7.2 198.0 %copy-start = (bf16[1,192,4096]{2,1,0:T(8,128)(2,1)S(1)}, bf16[1,192,4096]{2,1,0:T(8,128)(2,1)}, u32[]{:S(2)}) copy-start(bf16[1,192,4096]{2,1,0:T(8,128)(2,1)} %param.11) | copy-start | bytes 4718596
  7.2 198.0 %all-gather.5.cloned.1.call-start = ((), (), s32[]{:S(2)}) async-start(), calls=%async_computation.5 | async-start | bytes 10616832 | tf_op jit(solution)/shard_map/all_gather | solution.py:58
  73.0 2.7 copy-start.7
  75.7 252.2 %all-gather.3.cloned.1.call-start = ((), (), s32[]{:S(2)}) async-start(), calls=%async_computation.4 | async-start | bytes 10616832 | tf_op jit(solution)/shard_map/all_gather | solution.py:61
  136.5 76.7 %copy-start.2 = (bf16[1,192,4096]{2,1,0:T(8,128)(2,1)S(1)}, bf16[1,192,4096]{2,1,0:T(8,128)(2,1)}, u32[]{:S(2)}) copy-start(bf16[1,192,4096]{2,1,0:T(8,128)(2,1)} %param.12) | copy-start | bytes 4718596
  136.5 344.4 %reduce-scatter.2.cloned.1.call-start = ((), (), s32[]{:S(2)}) async-start(), calls=%async_computation.6 | async-start | bytes 10616832 | tf_op jit(solution)/shard_map/reduce_scatter | solution.py:69
  205.2 8.0 %copy-start.8 = (bf16[1152,4096]{1,0:T(8,128)(2,1)S(1)}, bf16[1152,4096]{1,0:T(8,128)(2,1)}, u32[]{:S(2)}) copy-start(bf16[1152,4096]{1,0:T(8,128)(2,1)} %all-gather.5.cloned.1.call-done) | copy-start | bytes 28311556
  335.9 7.9 %copy-start.3 = (bf16[1152,192]{0,1:T(8,128)(2,1)}, bf16[1152,192]{0,1:T(8,128)(2,1)S(1)}, u32[]{:S(2)}) copy-start(bf16[1152,192]{0,1:T(8,128)(2,1)S(1)} %get-tuple-element.5) | copy-start | bytes 1327108
  335.9 7.9 %copy-start.5 = (bf16[1152,192]{0,1:T(8,128)(2,1)}, bf16[1152,192]{0,1:T(8,128)(2,1)S(1)}, u32[]{:S(2)}) copy-start(bf16[1152,192]{0,1:T(8,128)(2,1)S(1)} %get-tuple-element.4) | copy-start | bytes 1327108
  483.5 7.1 %copy-start.6 = (bf16[1152,192]{0,1:T(8,128)(2,1)S(1)}, bf16[1152,192]{0,1:T(8,128)(2,1)}, u32[]{:S(2)}) copy-start(bf16[1152,192]{0,1:T(8,128)(2,1)} %copy-done.5) | copy-start | bytes 1327108
  483.5 55.0 %all-to-all-start.2 = ((bf16[16,9,4096]{2,1,0:T(8,128)(2,1)}), bf16[16,9,4096]{2,1,0:T(8,128)(2,1)}, u32[]{:S(2)}, u32[]{:S(2)}) async-start(bf16[16,9,4096]{2,1,0:T(8,128)(2,1)} %reshape.31), calls=%async_computation.3 | async-start | bytes 4194304 | tf_op jit(solution)/shard_map/all_to_all | solution.py:75
  490.6 7.2 %copy-start.4 = (bf16[1152,192]{0,1:T(8,128)(2,1)S(1)}, bf16[1152,192]{0,1:T(8,128)(2,1)}, u32[]{:S(2)}) copy-start(bf16[1152,192]{0,1:T(8,128)(2,1)} %copy-done.3) | copy-start | bytes 1327108
  490.6 14.4 %slice-start = ((s8[9437184]{0:T(1024)(128)(4,1)}), s8[4194304]{0:T(1024)(128)(4,1)S(1)}, s32[]{:S(2)}) async-start(s8[9437184]{0:T(1024)(128)(4,1)} %bitcast.44), calls=%async_computation.7 | async-start | bytes 8388608
  490.7 14.4 %slice-start.1 = ((s8[9437184]{0:T(1024)(128)(4,1)}), s8[4194304]{0:T(1024)(128)(4,1)S(1)}, s32[]{:S(2)}) async-start(s8[9437184]{0:T(1024)(128)(4,1)} %bitcast.44), calls=%async_computation.8 | async-start | bytes 8388608
  497.9 7.2 %slice-start.2 = ((s8[9437184]{0:T(1024)(128)(4,1)}), s8[1048576]{0:T(1024)(128)(4,1)S(1)}, s32[]{:S(2)}) async-start(s8[9437184]{0:T(1024)(128)(4,1)} %bitcast.44), calls=%async_computation.9 | async-start | bytes 2097152
  497.9 7.2 %copy-start.9 = (f32[1152,192]{0,1:T(8,128)S(1)}, f32[1152,192]{0,1:T(8,128)}, u32[]{:S(2)}) copy-start(f32[1152,192]{0,1:T(8,128)} %fusion.6) | copy-start | bytes 2654212
  497.9 7.2 %copy-start.10 = (f32[1152,192]{0,1:T(8,128)S(1)}, f32[1152,192]{0,1:T(8,128)}, u32[]{:S(2)}) copy-start(f32[1152,192]{0,1:T(8,128)} %fusion.9) | copy-start | bytes 2654212
  540.4 2.2 copy-start.1
Sparse Core Ops, SparseCore 0:
  75.8 129.3 all-gather.4
  208.3 119.5 all-gather.2
  354.6 126.2 reduce-scatter.1
where the time goes:
time: 554 us; the launch traced here: 549 us
  waiting for transfers between devices  335 us (60%)
  blocking collectives  112 us (20%)
  matrix products  56.5 us (10%)
  local copies, waits for them, and re-layouts  18.2 us (3%)
  between operations  13.9 us (3%)
  starting transfers between devices  7.36 us (1%)
  other arithmetic  5.63 us (1%)
    reduce_scatter x1, waiting for transfers between devices, local(): lax.psum_scatter((term + jnp.dot(up_grad, w_up, preferred_element_type=jn...  126 us
    all_gather x1, waiting for transfers between devices, local(): lax.all_gather(part_grads.reshape(experts * capacity, model_width), 'resp...  111 us
    all_gather x1, waiting for transfers between devices, local(): lax.all_gather(part_rows.reshape(experts * capacity, model_width), 'resp'...  68.4 us
    all_to_all x1, blocking collectives, local(): lax.all_to_all(send_rows.reshape(experts, capacity, model_width), 'expert...  58.6 us
    all_to_all x1, blocking collectives, local(): lax.all_to_all(send_grads.reshape(experts, capacity, model_width), 'exper...  53.4 us
    all_to_all x1, waiting for transfers between devices, local(): lax.all_to_all(own_sums.reshape(experts, capacity, model_width), 'expert'...  30.1 us
  transfers between devices with their start and end apart: 4, of which 4 were waited for; matrix products, arithmetic and copies ran while one was open for 7% of the time, Pallas kernels for 0%

commit v1 on v0

v1 whole, which is shorter than its diff:
```python
import jax
import jax.numpy as jnp
from jax import lax
from jax.experimental import pallas as pl
from jax.experimental.pallas import tpu as pltpu
from jax.sharding import PartitionSpec as P

MESH = pl.DeviceIdType.MESH
BF16 = jnp.bfloat16
F32 = jnp.float32

TOK = 128
D = 4096
NE = 16
CAP = 9
BLK = NE * CAP
FB = 192
ROWS = 4 * BLK
CH = 2048
LANES = 128
SLAB = CH // LANES
PACK = BLK * SLAB
TC = 512
NT = D // TC
PER = CH // TC


def nt_dot(a, b):
    return lax.dot_general(a, b, (((1,), (1,)), ((), ())), preferred_element_type=F32)


def nn_dot(a, b):
    return jnp.dot(a, b, preferred_element_type=F32)


def loop(n, body, first=0):
    def step(i, carry):
        body(i)
        return carry

    lax.fori_loop(first, n, step, 0)


def kernel(
    tok_hbm, cot_hbm, ids_ref, gw_ref, wg_hbm, wu_hbm, wd_hbm,
    tg_hbm, og_hbm, ou_hbm, od_hbm,
    tok, cot, pt, perm, wgu, wd, send, recv, stage, xa, ga,
    pre, hg, gu, hid, dt, tx, rtx, ty, rty, dsend, drecv, back, tg,
    load_sem, w_ssem, w_rsem, a_ssem, a_rsem, g_ssem, g_rsem,
    x_ssem, x_rsem, y_ssem, y_rsem, d_ssem, d_rsem, b_ssem, b_rsem,
    out_sem, tok_sem,
):
    resp = lax.axis_index("resp")
    me = lax.axis_index("expert")
    core = lax.axis_index("group")
    y = resp // 2
    x_hi = resp % 2
    side = (y + core) % 2
    x_peer = {"resp": y * 2 + (1 - x_hi)}
    y_peer = {"resp": ((y + 1 + 2 * side) % 4) * 2 + x_hi}
    w_peer = {"resp": ((y + 3 + 2 * side) % 4) * 2 + x_hi}

    def remote(src, dst, ssem, rsem, to):
        return pltpu.make_async_remote_copy(
            src_ref=src, dst_ref=dst, send_sem=ssem, recv_sem=rsem, device_id=to, device_id_type=MESH
        )

    loads = [
        pltpu.make_async_copy(tok_hbm, tok, load_sem.at[0]),
        pltpu.make_async_copy(cot_hbm, cot, load_sem.at[1]),
        pltpu.make_async_copy(wg_hbm.at[0], wgu.at[pl.ds(0, FB)], load_sem.at[2]),
        pltpu.make_async_copy(wu_hbm.at[0], wgu.at[pl.ds(2 * FB, FB)], load_sem.at[3]),
        pltpu.make_async_copy(wd_hbm.at[0], wd.at[pl.ds(0, FB)], load_sem.at[4]),
    ]
    for c in loads:
        c.start()

    barrier = pltpu.get_barrier_semaphore()
    for peer in (x_peer, y_peer, w_peer):
        pl.semaphore_signal(barrier, inc=1, device_id=peer, device_id_type=MESH)

    def greet(d):
        pl.semaphore_signal(barrier, inc=1, device_id={"expert": (me + d) % NE}, device_id_type=MESH)

    loop(NE, greet, 1)
    pl.semaphore_wait(barrier, NE + 2)

    w_copies = [
        remote(wg_hbm.at[0], wgu.at[pl.ds(FB, FB)], w_ssem.at[0], w_rsem.at[0], w_peer),
        remote(wu_hbm.at[0], wgu.at[pl.ds(3 * FB, FB)], w_ssem.at[1], w_rsem.at[1], w_peer),
        remote(wd_hbm.at[0], wd.at[pl.ds(FB, FB)], w_ssem.at[2], w_rsem.at[2], w_peer),
    ]
    for c in w_copies:
        c.start()

    ids = ids_ref[...]
    lane = lax.broadcasted_iota(jnp.int32, (TOK, LANES), 1)
    row = lax.broadcasted_iota(jnp.int32, (TOK, LANES), 0)
    onehot = jnp.where(ids == lane, 1.0, 0.0).astype(F32)
    lower = jnp.where(row > lane, 1.0, 0.0).astype(BF16)
    rank = jnp.sum(nn_dot(lower, onehot.astype(BF16)) * onehot, axis=1, keepdims=True)
    target = ids * CAP + rank.astype(jnp.int32)
    slot = lax.broadcasted_iota(jnp.int32, (TOK, 2 * LANES), 1)
    chosen = jnp.where(slot == target, 1.0, 0.0).astype(F32)
    pt[...] = chosen.astype(BF16)
    perm[...] = chosen.T.astype(BF16)

    def a2a(buf_s, buf_r, ssem, rsem, c, other, mine):
        return remote(
            buf_s.at[c, pl.ds(pl.multiple_of(other * BLK, 16), BLK)],
            buf_r.at[c, pl.ds(pl.multiple_of(mine * BLK, 16), BLK)],
            ssem.at[c, other],
            rsem.at[c, mine],
            {"expert": other},
        )

    def a2a_start(buf_s, buf_r, ssem, rsem, c):
        loop(NE, lambda d: a2a(buf_s, buf_r, ssem, rsem, c, (me + d) % NE, me).start(), 1)
        own = pl.ds(pl.multiple_of(me * BLK, 16), BLK)
        buf_r[c, own, :] = buf_s[c, own, :]

    def a2a_arrived(buf_s, buf_r, ssem, rsem, c):
        def arrived(d):
            src = (me + d) % NE
            a2a(buf_s, buf_r, ssem, rsem, c, src, src).wait_recv()

        loop(NE, arrived, 1)

    def a2a_sent(buf_s, buf_r, ssem, rsem, c):
        loop(NE, lambda d: a2a(buf_s, buf_r, ssem, rsem, c, (me + d) % NE, me).wait_send(), 1)

    def pack(buf, c):
        def part(i):
            r = pl.ds(pl.multiple_of(i * BLK, 16), BLK)
            buf[c, r, :] = stage[r, :].astype(BF16)

        loop(SLAB, part)

    def unpack(buf, c):
        def part(i):
            r = pl.ds(pl.multiple_of(i * BLK, 16), BLK)
            stage[r, :] = buf[c, r, :].astype(F32)

        loop(SLAB, part)

    for c in range(4):
        if c == 0:
            loads[0].wait()
        if c == 2:
            loads[1].wait()
        for k in range(SLAB):
            cols = pl.ds((c % 2) * CH + k * LANES, LANES)
            if c < 2:
                rows = tok[:, cols]
            else:
                rows = (gw_ref[...] * cot[:, cols].astype(F32)).astype(BF16)
            stage[pl.ds(k, BLK, stride=SLAB), :] = nn_dot(perm[pl.ds(0, BLK), :], rows)
        pack(send, c)
        a2a_start(send, recv, a_ssem, a_rsem, c)

    def gather(c, kind):
        buf = (xa, ga)[c // 2]
        cols = pl.ds((c % 2) * CH, CH)
        frm, to, peer = ((0, 2, x_peer), (0, 1, y_peer), (2, 3, y_peer))[kind]
        return remote(
            buf.at[pl.ds(frm * BLK, BLK), cols],
            buf.at[pl.ds(to * BLK, BLK), cols],
            g_ssem.at[c, kind],
            g_rsem.at[c, kind],
            peer,
        )

    def forward(c):
        gather(c, 0).wait_recv()
        gather(c, 2).start()

    for c in range(4):
        a2a_arrived(send, recv, a_ssem, a_rsem, c)
        unpack(recv, c)
        buf = (xa, ga)[c // 2]
        for k in range(SLAB):
            cols = pl.ds((c % 2) * CH + k * LANES, LANES)
            buf[pl.ds(0, BLK), cols] = stage[pl.ds(k, BLK, stride=SLAB), :].astype(BF16)
        gather(c, 0).start()
        gather(c, 1).start()
        if c > 0:
            forward(c - 1)
    forward(3)

    for c in loads[2:]:
        c.wait()
    for c in w_copies[:2]:
        c.wait_recv()

    pre[...] = jnp.zeros_like(pre)
    hg[...] = jnp.zeros_like(hg)
    for c in range(4):
        gather(c, 1).wait_recv()
        gather(c, 2).wait_recv()
        if c == 2:
            w_copies[2].wait_recv()
        buf, w, acc = ((xa, wgu, pre), (ga, wd, hg))[c // 2]

        def part(k, c=c, buf=buf, w=w, acc=acc):
            cols = pl.ds(pl.multiple_of((c % 2) * CH + k * TC, TC), TC)
            acc[...] += nt_dot(buf[:, cols], w[:, cols])

        loop(PER, part)

    def slopes(i):
        r = pl.ds(pl.multiple_of(i * 48, 16), 48)
        a = pre[r, 0 : 2 * FB]
        u = pre[r, 2 * FB : 4 * FB]
        h = hg[r, :]
        sig = jax.nn.sigmoid(a)
        act = a * sig
        hid[r, :] = (act * u).astype(BF16)
        gu[r, 0 : 2 * FB] = (h * u * (sig * (1.0 + a * (1.0 - sig)))).astype(BF16)
        gu[r, 2 * FB : 4 * FB] = (h * act).astype(BF16)

    loop(ROWS // 48, slopes)

    gut = gu[...].T
    hidt = hid[...].T
    dt[0:FB, :] = gut[FB : 2 * FB]
    dt[FB : 2 * FB, :] = gut[3 * FB : 4 * FB]
    dt[2 * FB : 3 * FB, :] = hidt[FB : 2 * FB]
    dt[3 * FB : 4 * FB, :] = gut[0:FB]
    dt[4 * FB : 5 * FB, :] = gut[2 * FB : 3 * FB]
    dt[5 * FB : 6 * FB, :] = hidt[0:FB]

    def tail_cols(j):
        return pl.ds(pl.multiple_of(j * TC, TC), TC)

    def x_sum(j):
        cols = tail_cols(j)
        return remote(tx.at[:, cols], rtx.at[:, cols], x_ssem.at[j], x_rsem.at[j], x_peer)

    def y_sum(j):
        cols = tail_cols(j)
        return remote(ty.at[:, cols], rty.at[:, cols], y_ssem.at[j], y_rsem.at[j], y_peer)

    def d_sum(j):
        cols = tail_cols(j)
        return remote(dsend.at[:, cols], drecv.at[:, cols], d_ssem.at[j], d_rsem.at[j], w_peer)

    def weights_out(j):
        cols = tail_cols(j)
        return [
            pltpu.make_async_copy(drecv.at[pl.ds(m * FB, FB), cols], o.at[0, :, cols], out_sem.at[m, j])
            for m, o in enumerate((og_hbm, ou_hbm, od_hbm))
        ]

    def other_weights(j):
        cols = tail_cols(j)
        dsend[0 : 2 * FB, cols] = nn_dot(dt[0 : 2 * FB, :], xa[:, cols]).astype(BF16)
        dsend[2 * FB : 3 * FB, cols] = nn_dot(dt[2 * FB : 3 * FB, :], ga[:, cols]).astype(BF16)
        d_sum(j).start()

    def own_weights(j):
        cols = tail_cols(j)
        d_sum(j).wait_recv()
        a = nn_dot(dt[3 * FB : 5 * FB, :], xa[:, cols])
        drecv[0 : 2 * FB, cols] = (a + drecv[0 : 2 * FB, cols].astype(F32)).astype(BF16)
        b = nn_dot(dt[5 * FB : 6 * FB, :], ga[:, cols])
        drecv[2 * FB : 3 * FB, cols] = (b + drecv[2 * FB : 3 * FB, cols].astype(F32)).astype(BF16)
        for c in weights_out(j):
            c.start()

    def x_part(j):
        cols = tail_cols(j)
        tx[:, cols] = nn_dot(gu[2 * BLK : 4 * BLK, :], wgu[:, cols]).astype(BF16)
        x_sum(j).start()

    def y_part(j):
        cols = tail_cols(j)
        x_sum(j).wait_recv()
        t = nn_dot(gu[BLK : 2 * BLK, :], wgu[:, cols])
        ty[:, cols] = (t + rtx[BLK : 2 * BLK, cols].astype(F32)).astype(BF16)
        y_sum(j).start()

    for c in range(4):
        a2a_sent(send, recv, a_ssem, a_rsem, c)

    def own_part(j):
        cols = tail_cols(j)
        y_sum(j).wait_recv()
        t = nn_dot(gu[0:BLK, :], wgu[:, cols])
        t = t + rtx[0:BLK, cols].astype(F32) + rty[:, cols].astype(F32)
        for i in range(TC // LANES):
            stage[pl.ds((j % PER) * (TC // LANES) + i, BLK, stride=SLAB), :] = t[:, i * LANES : (i + 1) * LANES]

        for b in range(2):

            @pl.when(j == b * PER + PER - 1)
            def _():
                pack(send, b)
                a2a_start(send, back, b_ssem, b_rsem, b)

    EARLY = 2
    LAG = 2

    def first(j):
        x_part(j)

        @pl.when(j < EARLY)
        def _():
            other_weights(j)

    loop(NT, first)

    def second(j):
        @pl.when(j < NT)
        def _():
            y_part(j)

        @pl.when(j + EARLY < NT)
        def _():
            other_weights(j + EARLY)

        @pl.when((j >= 1) & (j < NT + 1))
        def _():
            own_part(j - 1)

        @pl.when(j >= LAG)
        def _():
            own_weights(j - LAG)

    loop(NT + LAG, second)

    tg_out = [
        pltpu.make_async_copy(tg.at[:, pl.ds(b * CH, CH)], tg_hbm.at[:, pl.ds(b * CH, CH)], tok_sem.at[b])
        for b in range(2)
    ]
    for b in range(2):
        a2a_arrived(send, back, b_ssem, b_rsem, b)
        unpack(back, b)
        for k in range(SLAB):
            rows = stage[pl.ds(k, BLK, stride=SLAB), :].astype(BF16)
            tg[:, pl.ds(b * CH + k * LANES, LANES)] = nn_dot(pt[:, 0:BLK], rows).astype(BF16)
        tg_out[b].start()

    for c in w_copies:
        c.wait_send()
    for c in range(4):
        for kind in range(3):
            gather(c, kind).wait_send()
    for b in range(2):
        a2a_sent(send, back, b_ssem, b_rsem, b)

    def drain(j):
        x_sum(j).wait_send()
        y_sum(j).wait_send()
        d_sum(j).wait_send()
        for c in weights_out(j):
            c.wait()

    loop(NT, drain)
    for c in tg_out:
        c.wait()


def local(tokens, cotangent, expert_ids, gate_weights, gate_proj, up_proj, down_proj):
    hbm = pl.BlockSpec(memory_space=pl.ANY)
    vmem = pl.BlockSpec(memory_space=pltpu.VMEM)
    dma = pltpu.SemaphoreType.DMA
    wide = jax.ShapeDtypeStruct((1, FB, D), BF16)
    return pl.pallas_call(
        kernel,
        out_shape=(jax.ShapeDtypeStruct((TOK, D), BF16), wide, wide, wide),
        in_specs=[hbm, hbm, vmem, vmem, hbm, hbm, hbm],
        out_specs=(hbm, hbm, hbm, hbm),
        scratch_shapes=[
            pltpu.VMEM((TOK, D), BF16),
            pltpu.VMEM((TOK, D), BF16),
            pltpu.VMEM((TOK, 2 * LANES), BF16),
            pltpu.VMEM((2 * LANES, TOK), BF16),
            pltpu.VMEM((4 * FB, D), BF16),
            pltpu.VMEM((2 * FB, D), BF16),
            pltpu.VMEM((4, PACK, LANES), BF16),
            pltpu.VMEM((4, PACK, LANES), BF16),
            pltpu.VMEM((PACK, LANES), F32),
            pltpu.VMEM((ROWS, D), BF16),
            pltpu.VMEM((ROWS, D), BF16),
            pltpu.VMEM((ROWS, 4 * FB), F32),
            pltpu.VMEM((ROWS, 2 * FB), F32),
            pltpu.VMEM((ROWS, 4 * FB), BF16),
            pltpu.VMEM((ROWS, 2 * FB), BF16),
            pltpu.VMEM((6 * FB, ROWS), BF16),
            pltpu.VMEM((2 * BLK, D), BF16),
            pltpu.VMEM((2 * BLK, D), BF16),
            pltpu.VMEM((BLK, D), BF16),
            pltpu.VMEM((BLK, D), BF16),
            pltpu.VMEM((3 * FB, D), BF16),
            pltpu.VMEM((3 * FB, D), BF16),
            pltpu.VMEM((2, PACK, LANES), BF16),
            pltpu.VMEM((TOK, D), BF16),
            dma((5,)),
            dma((3,)),
            dma((3,)),
            dma((4, NE)),
            dma((4, NE)),
            dma((4, 3)),
            dma((4, 3)),
            dma((NT,)),
            dma((NT,)),
            dma((NT,)),
            dma((NT,)),
            dma((NT,)),
            dma((NT,)),
            dma((2, NE)),
            dma((2, NE)),
            dma((3, NT)),
            dma((2,)),
        ],
        cost_estimate=pl.CostEstimate(flops=14_500_000_000, bytes_accessed=12_500_000, transcendentals=300_000),
        compiler_params=pltpu.CompilerParams(
            collective_id=0, has_side_effects=True, vmem_limit_bytes=60 * 2**20
        ),
    )(tokens, cotangent, expert_ids, gate_weights, gate_proj, up_proj, down_proj)


def solution(mesh):
    rows = P(("group", "resp", "expert"), None)
    weights = P("expert", "resp", None)
    grads = P(("group", "expert"), "resp", None)
    return jax.shard_map(
        local,
        mesh=mesh,
        in_specs=(rows, rows, rows, rows, weights, weights, weights),
        out_specs=(rows, grads, grads, grads),
        check_vma=False,
    )
```

time: 554 us -> 213 us (0.38)
  waiting for transfers between devices: 335 us -> 0 us
  Pallas kernels: 0 us -> 199 us
  blocking collectives: 112 us -> 0 us
  matrix products: 56.5 us -> 0 us
  between operations: 13.9 us -> 0.65 us
  local copies, waits for them, and re-layouts: 18.2 us -> 10.3 us
  starting transfers between devices: 7.36 us -> 0 us
  other arithmetic: 5.63 us -> 0 us
    pallas_call x0 -> x1, Pallas kernels: none -> 199 us  [local(): pl.pallas_call(kernel, out_shape=(jax.ShapeDtypeStruct((TOK, D), BF16), w...]
    all_gather x2 -> x0, waiting for transfers between devices: 179 us -> none  [the longest x1 111 us: local(): lax.all_gather(part_grads.reshape(experts * capacity, model_width), 'resp...]
    reduce_scatter x1 -> x0, waiting for transfers between devices: 126 us -> none  [local(): lax.psum_scatter((term + jnp.dot(up_grad, w_up, preferred_element_type=jn...]
    all_to_all x2 -> x0, blocking collectives: 112 us -> none  [the longest x1 58.6 us: local(): lax.all_to_all(send_rows.reshape(experts, capacity, model_width), 'expert...]
    dot_general x8 -> x0, matrix products: 56.5 us -> none  [the longest x1 10.7 us: local(): jnp.dot(up_grad, w_up, preferred_element_type=jnp.float32)]
    all_to_all x1 -> x0, waiting for transfers between devices: 30.1 us -> none  [local(): lax.all_to_all(own_sums.reshape(experts, capacity, model_width), 'expert'...]
    reshape x6 -> x0, local copies, waits for them, and re-layouts: 12.9 us -> none  [the longest x1 2.64 us: local(): own_sums.reshape(experts, capacity, model_width)]
    unnamed x28 -> x12, local copies, waits for them, and re-layouts: 0.07 us -> 10.3 us
  transfers between devices with their start and end apart: 4 -> 0, of which waited for: 4 -> 0; matrix products, arithmetic and copies ran while one was open for 7% -> 0% of each run, Pallas kernels for 0% -> 0%
where the time goes in v1:
time: 213 us; the launch traced here: 210 us
  Pallas kernels  199 us (93%)
  local copies, waits for them, and re-layouts  10.3 us (5%)
    pallas_call x1, Pallas kernels, local(): pl.pallas_call(kernel, out_shape=(jax.ShapeDtypeStruct((TOK, D), BF16), w...  199 us
    unnamed x12, local copies, waits for them, and re-layouts  10.3 us

profile of v1, /device:TPU:25, one launch (start us, length us, event | category | flops | bytes accessed | tf_op | source)
XLA Modules:
  0.0 210.4 jit_solution(12149438939716357143)
XLA Ops:
  0.6 1.4 copy.11.ids_ref
  2.0 1.4 copy.12.gw_ref
  3.4 199.5 %shard_map.102 = (bf16[128,4096]{1,0:T(8,128)(2,1)}, bf16[1,192,4096]{2,1,0:T(8,128)(2,1)}, bf16[1,192,4096]{2,1,0:T(8,128)(2,1)}, bf16[1,192,4096]{2,1,0:T(8,128)(2,1)}) custom-call(bf16[128,4096]{1,0:T(8,128)(2,1)} %tok_hbm.1, bf16[128,4096]{1,0:T(8,128)(2,1)} %cot_hbm.1, s32[128,1]{1,0:T(8,128)} %copy.11.ids_ref, f32[128,1]{1,0:T(8,128)} %copy.12.gw_ref, ...), custom_call_target="tpu_custom_call" | custom-call | flops 14499999744 | bytes 12500000 | tf_op jit(solution)/shard_map/pallas_call | solution.py:368
  202.9 0.0 copy-start.2
  202.9 2.4 %copy.17 = bf16[128,4096]{1,0:T(8,128)(2,1)} copy(bf16[128,4096]{1,0:T(8,128)(2,1)} %get-tuple-element.8) | data formatting | bytes 2097152
  205.3 0.0 copy-done.2
  205.3 0.0 copy-start.1
  205.3 1.1 copy.18
  206.4 0.8 copy-done.1
  207.3 0.0 copy-start
  207.3 1.1 copy.19
  208.4 0.8 copy-done
  209.3 1.1 copy.20
Async XLA Ops:
  202.9 2.4 %copy-start.2 = (bf16[1,192,4096]{2,1,0:T(8,128)(2,1)S(1)}, bf16[1,192,4096]{2,1,0:T(8,128)(2,1)}, u32[]{:S(2)}) copy-start(bf16[1,192,4096]{2,1,0:T(8,128)(2,1)} %get-tuple-element.9) | copy-start | bytes 4718596
  205.3 2.0 copy-start.1
  207.3 2.0 copy-start

commit v2 on v1

v2 whole, which is shorter than its diff:
```python
import jax
import jax.numpy as jnp
from jax import lax
from jax.experimental import pallas as pl
from jax.experimental.pallas import tpu as pltpu
from jax.sharding import PartitionSpec as P

MESH = pl.DeviceIdType.MESH
BF16 = jnp.bfloat16
F32 = jnp.float32

TOK = 128
D = 4096
NE = 16
NZ = 8
CAP = 9
BLK = NE * CAP
HALF = NZ * CAP
FB = 192
ROWS = 4 * BLK
CH = 2048
LANES = 128
SLAB = CH // LANES
ZBLK = 2 * CAP * SLAB
EBLK = CAP * SLAB
GC = 1024
NG = D // GC
BSLAB = GC // LANES
BBLK = 2 * CAP * BSLAB
TC = 512
NT = D // TC
Y_FIRST = (1, 2)
EARLY = 8
LAG = 3


def nt_dot(a, b):
    return lax.dot_general(a, b, (((1,), (1,)), ((), ())), preferred_element_type=F32)


def nn_dot(a, b):
    return jnp.dot(a, b, preferred_element_type=F32)


def loop(n, body, first=0):
    def step(i, carry):
        body(i)
        return carry

    lax.fori_loop(first, n, step, 0)


def kernel(
    tok_hbm, cot_hbm, ids_ref, gw_ref, wg_hbm, wu_hbm, wd_hbm,
    tg_hbm, og_hbm, ou_hbm, od_hbm,
    tok, cot, pt, perm, order, wgu, wd, send, recv, over_y, over_x, over_yx, stage, xa, ga,
    pre, hg, gu, hid, dt, tx, rtx, kept, ty, rty, dsend, drecv, back,
    load_sem, w_ssem, w_rsem, a_ssem, a_rsem, p_ssem, p_rsem, q_ssem, q_rsem, g_ssem, g_rsem, h_ssem, h_rsem,
    x_ssem, x_rsem, y_ssem, y_rsem, d_ssem, d_rsem, e_ssem, e_rsem, b_ssem, b_rsem,
    out_sem, tok_sem,
):
    resp = lax.axis_index("resp")
    expert = lax.axis_index("expert")
    core = lax.axis_index("group")
    y = resp // 2
    z = expert // 2
    x_lo = expert % 2
    x = (resp % 2) * 2 + x_lo
    side = (y + core) % 2

    def at(y, x, z):
        return {"resp": y * 2 + x // 2, "expert": z * 2 + x % 2}

    y_peer = at((y + 1 + 2 * side) % 4, x, z)
    w_peer = at((y + 3 + 2 * side) % 4, x, z)
    x_peers = [at(y, (x + d) % 4, z) for d in (2, 1, 3)]
    lands = (0, 2, 1)

    def remote(src, dst, ssem, rsem, to):
        return pltpu.make_async_remote_copy(
            src_ref=src, dst_ref=dst, send_sem=ssem, recv_sem=rsem, device_id=to, device_id_type=MESH
        )

    loads = [
        pltpu.make_async_copy(tok_hbm, tok, load_sem.at[0]),
        pltpu.make_async_copy(cot_hbm, cot, load_sem.at[1]),
        pltpu.make_async_copy(wg_hbm.at[0], wgu.at[pl.ds(0, FB)], load_sem.at[2]),
        pltpu.make_async_copy(wu_hbm.at[0], wgu.at[pl.ds(2 * FB, FB)], load_sem.at[3]),
        pltpu.make_async_copy(wd_hbm.at[0], wd.at[pl.ds(0, FB)], load_sem.at[4]),
    ]
    for c in loads:
        c.start()

    barrier = pltpu.get_barrier_semaphore()
    for peer in [y_peer, w_peer] + x_peers:
        pl.semaphore_signal(barrier, inc=1, device_id=peer, device_id_type=MESH)

    def greet(d):
        pl.semaphore_signal(barrier, inc=1, device_id=at(y, x, (z + d) % NZ), device_id_type=MESH)

    loop(NZ, greet, 1)

    ids = ids_ref[...]
    ids = ids + x_lo * (1 - 2 * (ids & 1))
    lane = lax.broadcasted_iota(jnp.int32, (TOK, TOK), 1)
    row = lax.broadcasted_iota(jnp.int32, (TOK, TOK), 0)
    onehot = jnp.where(row == ids, 1.0, 0.0).astype(F32)
    upper = jnp.where(row < lane, 1.0, 0.0).astype(BF16)
    rank = jnp.sum(nn_dot(onehot.astype(BF16), upper) * onehot, axis=0, keepdims=True).astype(jnp.int32)
    slot = lax.broadcasted_iota(jnp.int32, (2 * LANES, TOK), 0)
    chosen = jnp.where(slot == ids * CAP + rank, 1.0, 0.0).astype(F32)
    perm[...] = chosen.astype(BF16)
    pt[...] = chosen.T.astype(BF16)
    scale = jnp.sum(chosen * gw_ref[...], axis=1, keepdims=True)[0:BLK]
    to = lax.broadcasted_iota(jnp.int32, (BLK, 2 * LANES), 0)
    frm = lax.broadcasted_iota(jnp.int32, (BLK, 2 * LANES), 1)
    to_z = (to * 57) >> 10
    rest = to - to_z * (2 * CAP)
    rest = jnp.where(rest >= CAP, rest - CAP + HALF, rest)
    order[...] = jnp.where(frm == rest + to_z * CAP, 1.0, 0.0).astype(BF16)

    def there(c, other, mine):
        return remote(
            send.at[c, other], recv.at[c, mine], a_ssem.at[c, other], a_rsem.at[c, mine], at(y, x, other)
        )

    def home(c, other, mine):
        return remote(
            send.at[c, other, pl.ds(0, BBLK)], back.at[c, mine], b_ssem.at[c, other], b_rsem.at[c, mine],
            at(y, x, other),
        )

    def a2a_start(way, c):
        loop(NZ, lambda d: way(c, (z + d) % NZ, z).start(), 1)

    def a2a_arrived(way, c):
        def arrived(d):
            src = (z + d) % NZ
            way(c, src, src).wait_recv()

        loop(NZ, arrived, 1)

    def a2a_sent(way, c):
        loop(NZ, lambda d: way(c, (z + d) % NZ, z).wait_send(), 1)

    def pack(c, rows):
        def part(i):
            send[c, i, pl.ds(0, rows), :] = stage[pl.ds(pl.multiple_of(i * rows, 16), rows), :].astype(BF16)

        loop(NZ, part)

    def dispatch(c):
        for k in range(SLAB):
            cols = pl.ds((c % 2) * CH + k * LANES, LANES)
            if c < 2:
                rows = nn_dot(perm[pl.ds(0, BLK), :], tok[:, cols])
            else:
                rows = nn_dot(perm[pl.ds(0, BLK), :], cot[:, cols]) * scale
            stage[pl.ds(k, BLK, stride=SLAB), :] = rows
        pack(c, ZBLK)

    def dispatched(c):
        a2a_start(there, c)
        recv[c, z] = send[c, z]

    loads[0].wait()
    dispatch(0)
    pl.semaphore_wait(barrier, NZ + 4)

    w_copies = [
        remote(wg_hbm.at[0], wgu.at[pl.ds(FB, FB)], w_ssem.at[0], w_rsem.at[0], w_peer),
        remote(wu_hbm.at[0], wgu.at[pl.ds(3 * FB, FB)], w_ssem.at[1], w_rsem.at[1], w_peer),
        remote(wd_hbm.at[0], wd.at[pl.ds(FB, FB)], w_ssem.at[2], w_rsem.at[2], w_peer),
    ]
    dispatched(0)
    for c in w_copies:
        c.start()
    for c in range(1, 4):
        if c == 2:
            loads[1].wait()
        dispatch(c)
        dispatched(c)

    def halves(ref, i):
        return ref.at[:, pl.ds(i * EBLK, EBLK)]

    def by_x(c, s):
        return remote(
            halves(recv.at[c], min(s, 1)), over_x.at[c, lands[s]], p_ssem.at[c, s], p_rsem.at[c, lands[s]],
            x_peers[s],
        )

    def by_yx(c, s):
        f = Y_FIRST.index(c)
        return remote(
            halves(over_y.at[f], min(s, 1)), over_yx.at[f, lands[s]], q_ssem.at[f, s], q_rsem.at[f, lands[s]],
            x_peers[s],
        )

    def by_y(c):
        f = Y_FIRST.index(c)
        return remote(recv.at[c], over_y.at[f], h_ssem.at[f], h_rsem.at[f], y_peer)

    def by_xy(p):
        buf = (xa, ga)[p // NG]
        cols = pl.ds((p % NG) * GC, GC)
        return remote(
            buf.at[pl.ds(0, 2 * BLK), cols], buf.at[pl.ds(2 * BLK, 2 * BLK), cols],
            g_ssem.at[p], g_rsem.at[p], y_peer,
        )

    def unpack(c, first, own, others):
        buf = (xa, ga)[c // 2]

        def part(i):
            for s in range(4):
                r = pl.ds(pl.multiple_of((s * NZ + i) * EBLK, 16), EBLK)
                if s == 0:
                    stage[r, :] = own[i, pl.ds(0, EBLK), :].astype(F32)
                else:
                    stage[r, :] = others[s - 1, i].astype(F32)

        loop(NZ, part)
        for k in range(SLAB):
            cols = pl.ds((c % 2) * CH + k * LANES, LANES)
            buf[pl.ds(first, 2 * BLK), cols] = stage[pl.ds(k, 2 * BLK, stride=SLAB), :].astype(BF16)

    def onward(c):
        if c in Y_FIRST:
            by_y(c).wait_recv()
            for s in range(3):
                by_yx(c, s).start()
        else:
            for s in range(3):
                by_x(c, s).wait_recv()
            unpack(c, 0, recv.at[c], over_x.at[c])
            for p in (2 * c, 2 * c + 1):
                by_xy(p).start()

    def settle(c):
        if c in Y_FIRST:
            f = Y_FIRST.index(c)
            for s in range(3):
                by_x(c, s).wait_recv()
            unpack(c, 0, recv.at[c], over_x.at[c])
            for s in range(3):
                by_yx(c, s).wait_recv()
            unpack(c, 2 * BLK, over_y.at[f], over_yx.at[f])
        else:
            for p in (2 * c, 2 * c + 1):
                by_xy(p).wait_recv()

    for c in range(4):
        a2a_arrived(there, c)
        if c in Y_FIRST:
            by_y(c).start()
        for s in range(3):
            by_x(c, s).start()
        if c > 0:
            onward(c - 1)
    onward(3)

    for c in loads[2:]:
        c.wait()
    for c in w_copies[:2]:
        c.wait_recv()

    def piece(p, w, acc):
        if p % 2 == 0:
            settle(p // 2)
        buf = (xa, ga)[p // NG]

        def part(k):
            cols = pl.ds(pl.multiple_of((p % NG) * GC + k * TC, TC), TC)
            t = nt_dot(buf[:, cols], w[:, cols])
            acc[...] = t + acc[...]

        loop(GC // TC, part)

    pre[...] = jnp.zeros_like(pre)
    hg[...] = jnp.zeros_like(hg)
    for p in range(NG):
        piece(p, wgu, pre)

    def activate(i):
        r = pl.ds(pl.multiple_of(i * 48, 16), 48)
        a = pre[r, 0 : 2 * FB]
        u = pre[r, 2 * FB : 4 * FB]
        sig = jax.nn.sigmoid(a)
        act = a * sig
        hid[r, :] = (act * u).astype(BF16)
        pre[r, 0 : 2 * FB] = u * (sig * (1.0 + a * (1.0 - sig)))
        pre[r, 2 * FB : 4 * FB] = act

    loop(ROWS // 48, activate)
    hidt = hid[...].T
    dt[2 * FB : 3 * FB, :] = hidt[FB : 2 * FB]
    dt[5 * FB : 6 * FB, :] = hidt[0:FB]

    w_copies[2].wait_recv()

    def e_sum(b):
        cols = pl.ds(pl.multiple_of(b * GC, GC), GC)
        rows = pl.ds(2 * FB, FB)
        return remote(dsend.at[rows, cols], drecv.at[rows, cols], e_ssem.at[b], e_rsem.at[b], w_peer)

    for p in range(NG, 2 * NG):
        piece(p, wd, hg)
        if p < 2 * NG - 1:
            cols = pl.ds((p % NG) * GC, GC)
            dsend[2 * FB : 3 * FB, cols] = nn_dot(dt[2 * FB : 3 * FB, :], ga[:, cols]).astype(BF16)
    for b in range(NG - 1):
        e_sum(b).start()

    def slopes(i):
        r = pl.ds(pl.multiple_of(i * 48, 16), 48)
        h = hg[r, :]
        gu[r, 0 : 2 * FB] = (h * pre[r, 0 : 2 * FB]).astype(BF16)
        gu[r, 2 * FB : 4 * FB] = (h * pre[r, 2 * FB : 4 * FB]).astype(BF16)

    loop(ROWS // 48, slopes)

    def tail_cols(j):
        return pl.ds(pl.multiple_of(j * TC, TC), TC)

    def outgoing(s):
        return wd.at[pl.ds(s * BLK, BLK)] if s < 2 else tx

    def x_sum(j, s):
        cols = tail_cols(j)
        return remote(
            outgoing(s).at[:, cols], rtx.at[lands[s], :, cols], x_ssem.at[j, s], x_rsem.at[j, lands[s]], x_peers[s]
        )

    def y_sum(j):
        cols = tail_cols(j)
        return remote(ty.at[:, cols], rty.at[:, cols], y_ssem.at[j], y_rsem.at[j], y_peer)

    def d_sum(j):
        cols = tail_cols(j)
        rows = pl.ds(0, 2 * FB)
        return remote(dsend.at[rows, cols], drecv.at[rows, cols], d_ssem.at[j], d_rsem.at[j], w_peer)

    def weights_out(j):
        cols = tail_cols(j)
        return [
            pltpu.make_async_copy(drecv.at[pl.ds(m * FB, FB), cols], o.at[0, :, cols], out_sem.at[m, j])
            for m, o in enumerate((og_hbm, ou_hbm, od_hbm))
        ]

    def other_weights(j):
        cols = tail_cols(j)
        dsend[0 : 2 * FB, cols] = nn_dot(dt[0 : 2 * FB, :], xa[:, cols]).astype(BF16)
        d_sum(j).start()

    def own_weights(j):
        cols = tail_cols(j)
        d_sum(j).wait_recv()
        a = nn_dot(dt[3 * FB : 5 * FB, :], xa[:, cols])
        drecv[0 : 2 * FB, cols] = (a + drecv[0 : 2 * FB, cols].astype(F32)).astype(BF16)
        @pl.when(j % 2 == 0)
        def _():
            e_sum(j // 2).wait_recv()

        b = nn_dot(dt[5 * FB : 6 * FB, :], ga[:, cols])
        drecv[2 * FB : 3 * FB, cols] = (b + drecv[2 * FB : 3 * FB, cols].astype(F32)).astype(BF16)
        for c in weights_out(j):
            c.start()

    def x_part(j):
        cols = tail_cols(j)
        t = nn_dot(gu[...], wgu[:, cols])

        def of(s):
            return jnp.concatenate(
                [t[s * HALF : (s + 1) * HALF], t[2 * BLK + s * HALF : 2 * BLK + (s + 1) * HALF]], axis=0
            ).astype(BF16)

        for s in range(3):
            outgoing(s)[:, cols] = of(s + 1)
            x_sum(j, s).start()
        kept[:, cols] = of(0)

    def sums(j, first):
        cols = tail_cols(j)
        a = kept[:, cols].astype(F32) + rtx[0, :, cols].astype(F32)
        b = rtx[1, :, cols].astype(F32) + rtx[2, :, cols].astype(F32)
        return jnp.concatenate([a[first : first + HALF], b[first : first + HALF]], axis=0)

    def y_part(j):
        for s in range(3):
            x_sum(j, s).wait_recv()
        ty[:, tail_cols(j)] = sums(j, HALF).astype(BF16)
        y_sum(j).start()

    for c in range(4):
        a2a_sent(there, c)
        for s in range(3):
            by_x(c, s).wait_send()
        if c in Y_FIRST:
            by_y(c).wait_send()

    def own_part(j):
        y_sum(j).wait_recv()
        t = sums(j, 0) + rty[:, tail_cols(j)].astype(F32)
        t = nn_dot(order[:, 0:BLK], t.astype(BF16))
        for i in range(TC // LANES):
            stage[pl.ds((j % 2) * (TC // LANES) + i, BLK, stride=BSLAB), :] = t[:, i * LANES : (i + 1) * LANES]

        @pl.when(j % 2 == 1)
        def _():
            b = j // 2
            pack(b, BBLK)
            a2a_start(home, b)
            back[b, z] = send[b, z, pl.ds(0, BBLK), :]

    loop(NT, x_part)

    cols = pl.ds((NG - 1) * GC, GC)
    dsend[2 * FB : 3 * FB, cols] = nn_dot(dt[2 * FB : 3 * FB, :], ga[:, cols]).astype(BF16)
    e_sum(NG - 1).start()
    gut = gu[...].T
    dt[0:FB, :] = gut[FB : 2 * FB]
    dt[FB : 2 * FB, :] = gut[3 * FB : 4 * FB]
    dt[3 * FB : 4 * FB, :] = gut[0:FB]
    dt[4 * FB : 5 * FB, :] = gut[2 * FB : 3 * FB]
    loop(EARLY, other_weights)

    def second(j):
        @pl.when(j < NT)
        def _():
            y_part(j)

        @pl.when(j + EARLY < NT)
        def _():
            other_weights(j + EARLY)

        @pl.when((j >= 1) & (j < NT + 1))
        def _():
            own_part(j - 1)

        @pl.when(j >= LAG)
        def _():
            own_weights(j - LAG)

    loop(NT + LAG, second)

    def tokens_out(b):
        cols = pl.ds(b * GC, GC)
        return pltpu.make_async_copy(tok.at[:, cols], tg_hbm.at[:, cols], tok_sem.at[b])

    for b in range(NG):
        a2a_arrived(home, b)

        def part(i, b=b):
            stage[pl.ds(pl.multiple_of(i * BBLK, 16), BBLK), :] = back[b, i].astype(F32)

        loop(NZ, part)
        for k in range(BSLAB):
            rows = stage[pl.ds(k, BLK, stride=BSLAB), :].astype(BF16)
            tok[:, pl.ds(b * GC + k * LANES, LANES)] = nn_dot(pt[:, 0:BLK], rows).astype(BF16)
        tokens_out(b).start()

    for c in w_copies:
        c.wait_send()
    for c in range(4):
        if c in Y_FIRST:
            for s in range(3):
                by_yx(c, s).wait_send()
        else:
            for p in (2 * c, 2 * c + 1):
                by_xy(p).wait_send()
    for b in range(NG):
        a2a_sent(home, b)
        e_sum(b).wait_send()

    def drain(j):
        for s in range(3):
            x_sum(j, s).wait_send()
        y_sum(j).wait_send()
        d_sum(j).wait_send()
        for c in weights_out(j):
            c.wait()

    loop(NT, drain)
    for b in range(NG):
        tokens_out(b).wait()


def copy_out(*refs):
    src, dst, held = refs[0:4], refs[4:8], refs[8:12]
    in_sem, out_sem = refs[12:]

    def parts(a, i):
        n = held[a].shape[0] // 4
        r = pl.ds(i * n, n)
        at = (r,) if a == 0 else (0, r)
        return (
            pltpu.make_async_copy(src[a].at[at], held[a].at[r], in_sem.at[a, i]),
            pltpu.make_async_copy(held[a].at[r], dst[a].at[at], out_sem.at[a, i]),
        )

    every = [parts(a, i) for a in range(4) for i in range(4)]
    for c, _ in every:
        c.start()
    for c, d in every:
        c.wait()
        d.start()
    for _, d in every:
        d.wait()


def local(tokens, cotangent, expert_ids, gate_weights, gate_proj, up_proj, down_proj):
    hbm = pl.BlockSpec(memory_space=pl.ANY)
    vmem = pl.BlockSpec(memory_space=pltpu.VMEM)
    dma = pltpu.SemaphoreType.DMA
    wide = jax.ShapeDtypeStruct((1, FB, D), BF16)
    outs = (jax.ShapeDtypeStruct((TOK, D), BF16), wide, wide, wide)
    done = pl.pallas_call(
        kernel,
        out_shape=outs,
        in_specs=[hbm, hbm, vmem, vmem, hbm, hbm, hbm],
        out_specs=(hbm, hbm, hbm, hbm),
        scratch_shapes=[
            pltpu.VMEM((TOK, D), BF16),
            pltpu.VMEM((TOK, D), BF16),
            pltpu.VMEM((TOK, 2 * LANES), BF16),
            pltpu.VMEM((2 * LANES, TOK), BF16),
            pltpu.VMEM((BLK, 2 * LANES), BF16),
            pltpu.VMEM((4 * FB, D), BF16),
            pltpu.VMEM((2 * FB, D), BF16),
            pltpu.VMEM((4, NZ, ZBLK, LANES), BF16),
            pltpu.VMEM((4, NZ, ZBLK, LANES), BF16),
            pltpu.VMEM((len(Y_FIRST), NZ, ZBLK, LANES), BF16),
            pltpu.VMEM((4, 3, NZ, EBLK, LANES), BF16),
            pltpu.VMEM((len(Y_FIRST), 3, NZ, EBLK, LANES), BF16),
            pltpu.VMEM((4 * NZ * EBLK, LANES), F32),
            pltpu.VMEM((ROWS, D), BF16),
            pltpu.VMEM((ROWS, D), BF16),
            pltpu.VMEM((ROWS, 4 * FB), F32),
            pltpu.VMEM((ROWS, 2 * FB), F32),
            pltpu.VMEM((ROWS, 4 * FB), BF16),
            pltpu.VMEM((ROWS, 2 * FB), BF16),
            pltpu.VMEM((6 * FB, ROWS), BF16),
            pltpu.VMEM((BLK, D), BF16),
            pltpu.VMEM((3, BLK, D), BF16),
            pltpu.VMEM((BLK, D), BF16),
            pltpu.VMEM((BLK, D), BF16),
            pltpu.VMEM((BLK, D), BF16),
            pltpu.VMEM((3 * FB, D), BF16),
            pltpu.VMEM((3 * FB, D), BF16),
            pltpu.VMEM((NG, NZ, BBLK, LANES), BF16),
            dma((5,)),
            dma((3,)),
            dma((3,)),
            dma((4, NZ)),
            dma((4, NZ)),
            dma((4, 3)),
            dma((4, 3)),
            dma((len(Y_FIRST), 3)),
            dma((len(Y_FIRST), 3)),
            dma((2 * NG,)),
            dma((2 * NG,)),
            dma((len(Y_FIRST),)),
            dma((len(Y_FIRST),)),
            dma((NT, 3)),
            dma((NT, 3)),
            dma((NT,)),
            dma((NT,)),
            dma((NT,)),
            dma((NT,)),
            dma((NG,)),
            dma((NG,)),
            dma((NG, NZ)),
            dma((NG, NZ)),
            dma((3, NT)),
            dma((NG,)),
        ],
        cost_estimate=pl.CostEstimate(flops=14_500_000_000, bytes_accessed=12_500_000, transcendentals=300_000),
        compiler_params=pltpu.CompilerParams(
            collective_id=0, has_side_effects=True, vmem_limit_bytes=62 * 2**20
        ),
    )(
        tokens, cotangent, expert_ids.reshape(1, TOK), gate_weights.reshape(1, TOK),
        gate_proj, up_proj, down_proj,
    )
    return pl.pallas_call(
        copy_out,
        out_shape=outs,
        in_specs=[hbm] * 4,
        out_specs=(hbm,) * 4,
        scratch_shapes=[pltpu.VMEM((TOK, D), BF16)] + [pltpu.VMEM((FB, D), BF16)] * 3 + [dma((4, 4)), dma((4, 4))],
    )(*done)


def solution(mesh):
    rows = P(("group", "resp", "expert"), None)
    weights = P("expert", "resp", None)
    grads = P(("group", "expert"), "resp", None)
    return jax.shard_map(
        local,
        mesh=mesh,
        in_specs=(rows, rows, rows, rows, weights, weights, weights),
        out_specs=(rows, grads, grads, grads),
        check_vma=False,
    )
```

time: 213 us -> 190 us (0.89)
  Pallas kernels: 199 us -> 185 us
  local copies, waits for them, and re-layouts: 10.3 us -> 0 us
    pallas_call x1 -> x2, Pallas kernels: 199 us -> 185 us  [the longest x1 180 us: local(): pl.pallas_call(kernel, out_shape=outs, in_specs=[hbm, hbm, vmem, vmem, hb...]
    unnamed x12 -> x0, local copies, waits for them, and re-layouts: 10.3 us -> none
where the time goes in v2:
time: 190 us; the launch traced here: 186 us
  Pallas kernels  185 us (97%)
    pallas_call x1, Pallas kernels, local(): pl.pallas_call(kernel, out_shape=outs, in_specs=[hbm, hbm, vmem, vmem, hb...  180 us
    pallas_call x1, Pallas kernels, local(): pl.pallas_call(copy_out, out_shape=outs, in_specs=[hbm] * 4, out_specs=(h...  5.15 us

profile of v2, /device:TPU:25, one launch (start us, length us, event | category | flops | bytes accessed | tf_op | source)
XLA Modules:
  0.0 186.2 jit_solution(11321593815505828707)
XLA Ops:
  0.6 180.2 %shard_map.102 = (bf16[128,4096]{1,0:T(8,128)(2,1)}, bf16[1,192,4096]{2,1,0:T(8,128)(2,1)}, bf16[1,192,4096]{2,1,0:T(8,128)(2,1)}, bf16[1,192,4096]{2,1,0:T(8,128)(2,1)}) custom-call(bf16[128,4096]{1,0:T(8,128)(2,1)} %tok_hbm.1, bf16[128,4096]{1,0:T(8,128)(2,1)} %cot_hbm.1, s32[1,128]{1,0:T(1,128)} %bitcast.2, f32[1,128]{1,0:T(1,128)} %bitcast.3, ...), custom_call_target="tpu_custom_call" | custom-call | flops 14499999744 | bytes 12500000 | tf_op jit(solution)/shard_map/pallas_call | solution.py:519
  180.9 5.2 %shard_map.103 = (bf16[128,4096]{1,0:T(8,128)(2,1)}, bf16[1,192,4096]{2,1,0:T(8,128)(2,1)}, bf16[1,192,4096]{2,1,0:T(8,128)(2,1)}, bf16[1,192,4096]{2,1,0:T(8,128)(2,1)}) custom-call(bf16[128,4096]{1,0:T(8,128)(2,1)} %get-tuple-element.8.refs_0_, bf16[1,192,4096]{2,1,0:T(8,128)(2,1)} %get-tuple-element.9.refs_1_, ...), custom_call_target="tpu_custom_call" | custom-call | tf_op jit(solution)/shard_map/pallas_call | solution.py:587

commit v3 on v2

--- a/solution.py
+++ b/solution.py
@@ -30,6 +30,7 @@
 TC = 512
 NT = D // TC
 Y_FIRST = (1, 2)
+EARLY_DOWN = 2
 EARLY = 8
 LAG = 3
 
@@ -53,9 +54,9 @@
 def kernel(
     tok_hbm, cot_hbm, ids_ref, gw_ref, wg_hbm, wu_hbm, wd_hbm,
     tg_hbm, og_hbm, ou_hbm, od_hbm,
-    tok, cot, pt, perm, order, wgu, wd, send, recv, over_y, over_x, over_yx, stage, xa, ga,
+    tok, cot, pt, perm, order, wgu, wd, send, recv, ahead, over_y, over_x, over_yx, stage, xa, ga,
     pre, hg, gu, hid, dt, tx, rtx, kept, ty, rty, dsend, drecv, back,
-    load_sem, w_ssem, w_rsem, a_ssem, a_rsem, p_ssem, p_rsem, q_ssem, q_rsem, g_ssem, g_rsem, h_ssem, h_rsem,
+    load_sem, w_ssem, w_rsem, a_ssem, a_rsem, f_ssem, f_rsem, p_ssem, p_rsem, q_ssem, q_rsem, g_ssem, g_rsem, h_ssem, h_rsem,
     x_ssem, x_rsem, y_ssem, y_rsem, d_ssem, d_rsem, e_ssem, e_rsem, b_ssem, b_rsem,
     out_sem, tok_sem,
 ):
@@ -143,6 +144,21 @@
     def a2a_sent(way, c):
         loop(NZ, lambda d: way(c, (z + d) % NZ, z).wait_send(), 1)
 
+    def halves(ref, i):
+        return ref.at[:, pl.ds(i * EBLK, EBLK)]
+
+    def ahead_x(s):
+        return remote(
+            halves(send.at[0], min(s, 1)), ahead.at[lands[s]], p_ssem.at[0, s], p_rsem.at[0, lands[s]], x_peers[s]
+        )
+
+    def ahead_z(s, other, mine):
+        if s == 0:
+            src, dst = send.at[0, other, pl.ds(0, EBLK)], recv.at[0, mine, pl.ds(0, EBLK)]
+        else:
+            src, dst = ahead.at[s - 1, other], over_x.at[0, s - 1, mine]
+        return remote(src, dst, f_ssem.at[s, other], f_rsem.at[s, mine], at(y, x, other))
+
     def pack(c, rows):
         def part(i):
             send[c, i, pl.ds(0, rows), :] = stage[pl.ds(pl.multiple_of(i * rows, 16), rows), :].astype(BF16)
@@ -172,7 +188,10 @@
         remote(wu_hbm.at[0], wgu.at[pl.ds(3 * FB, FB)], w_ssem.at[1], w_rsem.at[1], w_peer),
         remote(wd_hbm.at[0], wd.at[pl.ds(FB, FB)], w_ssem.at[2], w_rsem.at[2], w_peer),
     ]
-    dispatched(0)
+    for s in range(3):
+        ahead_x(s).start()
+    a2a_start(ahead_z, 0)
+    recv[0, z, pl.ds(0, EBLK), :] = send[0, z, pl.ds(0, EBLK), :]
     for c in w_copies:
         c.start()
     for c in range(1, 4):
@@ -181,8 +200,10 @@
         dispatch(c)
         dispatched(c)
 
-    def halves(ref, i):
-        return ref.at[:, pl.ds(i * EBLK, EBLK)]
+    for s in range(3):
+        ahead_x(s).wait_recv()
+        a2a_start(ahead_z, lands[s] + 1)
+        over_x[0, lands[s], z] = ahead[lands[s], z]
 
     def by_x(c, s):
         return remote(
@@ -231,8 +252,11 @@
             for s in range(3):
                 by_yx(c, s).start()
         else:
-            for s in range(3):
-                by_x(c, s).wait_recv()
+            for s in range(4):
+                if c == 0:
+                    a2a_arrived(ahead_z, s)
+                elif s < 3:
+                    by_x(c, s).wait_recv()
             unpack(c, 0, recv.at[c], over_x.at[c])
             for p in (2 * c, 2 * c + 1):
                 by_xy(p).start()
@@ -250,14 +274,15 @@
             for p in (2 * c, 2 * c + 1):
                 by_xy(p).wait_recv()
 
-    for c in range(4):
+    for c in range(1, 4):
         a2a_arrived(there, c)
         if c in Y_FIRST:
             by_y(c).start()
         for s in range(3):
             by_x(c, s).start()
-        if c > 0:
+        if c > 1:
             onward(c - 1)
+    onward(0)
     onward(3)
 
     for c in loads[2:]:
@@ -309,7 +334,9 @@
         if p < 2 * NG - 1:
             cols = pl.ds((p % NG) * GC, GC)
             dsend[2 * FB : 3 * FB, cols] = nn_dot(dt[2 * FB : 3 * FB, :], ga[:, cols]).astype(BF16)
-    for b in range(NG - 1):
+            if p - NG < EARLY_DOWN:
+                e_sum(p - NG).start()
+    for b in range(EARLY_DOWN, NG - 1):
         e_sum(b).start()
 
     def slopes(i):
@@ -393,7 +420,11 @@
         ty[:, tail_cols(j)] = sums(j, HALF).astype(BF16)
         y_sum(j).start()
 
-    for c in range(4):
+    for s in range(4):
+        a2a_sent(ahead_z, s)
+    for s in range(3):
+        ahead_x(s).wait_send()
+    for c in range(1, 4):
         a2a_sent(there, c)
         for s in range(3):
             by_x(c, s).wait_send()
@@ -531,6 +562,7 @@
             pltpu.VMEM((2 * FB, D), BF16),
             pltpu.VMEM((4, NZ, ZBLK, LANES), BF16),
             pltpu.VMEM((4, NZ, ZBLK, LANES), BF16),
+            pltpu.VMEM((3, NZ, EBLK, LANES), BF16),
             pltpu.VMEM((len(Y_FIRST), NZ, ZBLK, LANES), BF16),
             pltpu.VMEM((4, 3, NZ, EBLK, LANES), BF16),
             pltpu.VMEM((len(Y_FIRST), 3, NZ, EBLK, LANES), BF16),
@@ -553,6 +585,8 @@
             dma((5,)),
             dma((3,)),
             dma((3,)),
+            dma((4, NZ)),
+            dma((4, NZ)),
             dma((4, NZ)),
             dma((4, NZ)),
             dma((4, 3)),

time: 190 us -> 186 us (0.979); the launches traced: 186 us -> 186 us
  no operation moved by 1% of the time
where the time goes in v3:
time: 186 us
  Pallas kernels  185 us (99%)
    pallas_call x1, Pallas kernels, local(): pl.pallas_call(kernel, out_shape=outs, in_specs=[hbm, hbm, vmem, vmem, hb...  180 us
    pallas_call x1, Pallas kernels, local(): pl.pallas_call(copy_out, out_shape=outs, in_specs=[hbm] * 4, out_specs=(h...  5.15 us

profile of v3, /device:TPU:25, one launch (start us, length us, event | category | flops | bytes accessed | tf_op | source)
XLA Modules:
  0.0 185.9 jit_solution(8777379311259223354)
XLA Ops:
  0.6 179.9 %shard_map.102 = (bf16[128,4096]{1,0:T(8,128)(2,1)}, bf16[1,192,4096]{2,1,0:T(8,128)(2,1)}, bf16[1,192,4096]{2,1,0:T(8,128)(2,1)}, bf16[1,192,4096]{2,1,0:T(8,128)(2,1)}) custom-call(bf16[128,4096]{1,0:T(8,128)(2,1)} %tok_hbm.1, bf16[128,4096]{1,0:T(8,128)(2,1)} %cot_hbm.1, s32[1,128]{1,0:T(1,128)} %bitcast.2, f32[1,128]{1,0:T(1,128)} %bitcast.3, ...), custom_call_target="tpu_custom_call" | custom-call | flops 14499999744 | bytes 12500000 | tf_op jit(solution)/shard_map/pallas_call | solution.py:550
  180.5 5.2 %shard_map.103 = (bf16[128,4096]{1,0:T(8,128)(2,1)}, bf16[1,192,4096]{2,1,0:T(8,128)(2,1)}, bf16[1,192,4096]{2,1,0:T(8,128)(2,1)}, bf16[1,192,4096]{2,1,0:T(8,128)(2,1)}) custom-call(bf16[128,4096]{1,0:T(8,128)(2,1)} %get-tuple-element.8.refs_0_, bf16[1,192,4096]{2,1,0:T(8,128)(2,1)} %get-tuple-element.9.refs_1_, ...), custom_call_target="tpu_custom_call" | custom-call | tf_op jit(solution)/shard_map/pallas_call | solution.py:621

commit v4 on v3

--- a/solution.py
+++ b/solution.py
@@ -30,8 +30,9 @@
 TC = 512
 NT = D // TC
 Y_FIRST = (1, 2)
-EARLY_DOWN = 2
+EARLY_DOWN = 3
 EARLY = 8
+HEAD = 2
 LAG = 3
 
 
@@ -445,7 +446,7 @@
             a2a_start(home, b)
             back[b, z] = send[b, z, pl.ds(0, BBLK), :]
 
-    loop(NT, x_part)
+    loop(HEAD, x_part)
 
     cols = pl.ds((NG - 1) * GC, GC)
     dsend[2 * FB : 3 * FB, cols] = nn_dot(dt[2 * FB : 3 * FB, :], ga[:, cols]).astype(BF16)
@@ -455,7 +456,9 @@
     dt[FB : 2 * FB, :] = gut[3 * FB : 4 * FB]
     dt[3 * FB : 4 * FB, :] = gut[0:FB]
     dt[4 * FB : 5 * FB, :] = gut[2 * FB : 3 * FB]
-    loop(EARLY, other_weights)
+    loop(HEAD, other_weights)
+    loop(NT, x_part, HEAD)
+    loop(EARLY, other_weights, HEAD)
 
     def second(j):
         @pl.when(j < NT)

time: 186 us -> 186 us (level)
  no operation moved by 1% of the time
where the time goes in v4:
time: 186 us
  Pallas kernels  185 us (99%)
    pallas_call x1, Pallas kernels, local(): pl.pallas_call(kernel, out_shape=outs, in_specs=[hbm, hbm, vmem, vmem, hb...  180 us
    pallas_call x1, Pallas kernels, local(): pl.pallas_call(copy_out, out_shape=outs, in_specs=[hbm] * 4, out_specs=(h...  5.15 us

profile of v4, /device:TPU:25, one launch (start us, length us, event | category | flops | bytes accessed | tf_op | source)
XLA Modules:
  0.0 185.9 jit_solution(1042532440073810895)
XLA Ops:
  0.6 179.9 %shard_map.102 = (bf16[128,4096]{1,0:T(8,128)(2,1)}, bf16[1,192,4096]{2,1,0:T(8,128)(2,1)}, bf16[1,192,4096]{2,1,0:T(8,128)(2,1)}, bf16[1,192,4096]{2,1,0:T(8,128)(2,1)}) custom-call(bf16[128,4096]{1,0:T(8,128)(2,1)} %tok_hbm.1, bf16[128,4096]{1,0:T(8,128)(2,1)} %cot_hbm.1, s32[1,128]{1,0:T(1,128)} %bitcast.2, f32[1,128]{1,0:T(1,128)} %bitcast.3, ...), custom_call_target="tpu_custom_call" | custom-call | flops 14499999744 | bytes 12500000 | tf_op jit(solution)/shard_map/pallas_call | solution.py:553
  180.5 5.2 %shard_map.103 = (bf16[128,4096]{1,0:T(8,128)(2,1)}, bf16[1,192,4096]{2,1,0:T(8,128)(2,1)}, bf16[1,192,4096]{2,1,0:T(8,128)(2,1)}, bf16[1,192,4096]{2,1,0:T(8,128)(2,1)}) custom-call(bf16[128,4096]{1,0:T(8,128)(2,1)} %get-tuple-element.8.refs_0_, bf16[1,192,4096]{2,1,0:T(8,128)(2,1)} %get-tuple-element.9.refs_1_, ...), custom_call_target="tpu_custom_call" | custom-call | tf_op jit(solution)/shard_map/pallas_call | solution.py:624

commit v5 on v4

--- a/solution.py
+++ b/solution.py
@@ -28,6 +28,7 @@
 BSLAB = GC // LANES
 BBLK = 2 * CAP * BSLAB
 TC = 512
+PART = 32
 NT = D // TC
 Y_FIRST = (1, 2)
 EARLY_DOWN = 3
@@ -526,15 +527,14 @@
     in_sem, out_sem = refs[12:]
 
     def parts(a, i):
-        n = held[a].shape[0] // 4
-        r = pl.ds(i * n, n)
+        r = pl.ds(i * PART, PART)
         at = (r,) if a == 0 else (0, r)
         return (
             pltpu.make_async_copy(src[a].at[at], held[a].at[r], in_sem.at[a, i]),
             pltpu.make_async_copy(held[a].at[r], dst[a].at[at], out_sem.at[a, i]),
         )
 
-    every = [parts(a, i) for a in range(4) for i in range(4)]
+    every = [parts(a, i) for a in range(4) for i in range(held[a].shape[0] // PART)]
     for c, _ in every:
         c.start()
     for c, d in every:
@@ -626,7 +626,7 @@
         out_shape=outs,
         in_specs=[hbm] * 4,
         out_specs=(hbm,) * 4,
-        scratch_shapes=[pltpu.VMEM((TOK, D), BF16)] + [pltpu.VMEM((FB, D), BF16)] * 3 + [dma((4, 4)), dma((4, 4))],
+        scratch_shapes=[pltpu.VMEM((TOK, D), BF16)] + [pltpu.VMEM((FB, D), BF16)] * 3 + [dma((4, FB // PART))] * 2,
     )(*done)
 
 

time: 186 us -> 186 us (level)
  no operation moved by 1% of the time
where the time goes in v5:
time: 186 us
  Pallas kernels  185 us (99%)
    pallas_call x1, Pallas kernels, local(): pl.pallas_call(kernel, out_shape=outs, in_specs=[hbm, hbm, vmem, vmem, hb...  180 us
    pallas_call x1, Pallas kernels, local(): pl.pallas_call(copy_out, out_shape=outs, in_specs=[hbm] * 4, out_specs=(h...  5.33 us

profile of v5, /device:TPU:25, one launch (start us, length us, event | category | flops | bytes accessed | tf_op | source)
XLA Modules:
  0.0 186.0 jit_solution(5298945294578885927)
XLA Ops:
  0.6 179.9 %shard_map.102 = (bf16[128,4096]{1,0:T(8,128)(2,1)}, bf16[1,192,4096]{2,1,0:T(8,128)(2,1)}, bf16[1,192,4096]{2,1,0:T(8,128)(2,1)}, bf16[1,192,4096]{2,1,0:T(8,128)(2,1)}) custom-call(bf16[128,4096]{1,0:T(8,128)(2,1)} %tok_hbm.1, bf16[128,4096]{1,0:T(8,128)(2,1)} %cot_hbm.1, s32[1,128]{1,0:T(1,128)} %bitcast.2, f32[1,128]{1,0:T(1,128)} %bitcast.3, ...), custom_call_target="tpu_custom_call" | custom-call | flops 14499999744 | bytes 12500000 | tf_op jit(solution)/shard_map/pallas_call | solution.py:553
  180.5 5.3 %shard_map.103 = (bf16[128,4096]{1,0:T(8,128)(2,1)}, bf16[1,192,4096]{2,1,0:T(8,128)(2,1)}, bf16[1,192,4096]{2,1,0:T(8,128)(2,1)}, bf16[1,192,4096]{2,1,0:T(8,128)(2,1)}) custom-call(bf16[128,4096]{1,0:T(8,128)(2,1)} %get-tuple-element.8.refs_0_, bf16[1,192,4096]{2,1,0:T(8,128)(2,1)} %get-tuple-element.9.refs_1_, ...), custom_call_target="tpu_custom_call" | custom-call | tf_op jit(solution)/shard_map/pallas_call | solution.py:624
